TPU v7x, 32 devices: a whole 2x2x4 slice. The times are simulated.
32 devices in a mesh: pipe: 2 (over x), ctx: 4 (over y, core), dp: 4 (over z).
Axes of the slice: x: 2, y: 2, z: 4, core: 2. Of those that a mesh axis runs over, the one named last changes fastest.
Arguments:
- patches: bfloat16 [1, 4, 512, 1024], P(None, 'dp', 'ctx'), may hold values from -6 to 6
- lengths: int32 [1, 4], P(None, 'dp'), may hold values from 128 to 512, as said below
- norm_gain: float32 [2, 1024], P('pipe'), may hold values from 0.1 to 1.9
- norm_bias: float32 [2, 1024], P('pipe'), may hold values from -3 to 3
- w_qkv: bfloat16 [2, 1024, 3072], P('pipe', None, 'dp')
- w_out: bfloat16 [2, 1024, 1024], P('pipe'), may hold values from -0.1875 to 0.1875
- out_bias: float32 [2, 1024], P('pipe'), may hold values from -3 to 3
- scale_gain: float32 [2, 1024], P('pipe'), may hold values from 0.3 to 1.5
Outputs:
- section_outputs: bfloat16 [2, 1, 4, 512, 1024], P('pipe', None, 'dp', 'ctx')
Inputs may be any that keep to these rules, and one draw needn't show every extreme that they name: `lengths`: every volume has at least 128 real tokens, and in every draw some volume fills all 512 slots.
All inputs are finite; a program needn't handle non-finite values.
Results may differ from a plain program's by a relative error of at most 0.017.
The roundings to bfloat16 on the way count: a program that leaves them out, or rounds other values in their place, can miss the bound.
Values may be sent and summed in bfloat16 or wider, within the bound.
A program may use at most 128 MiB of HBM per device.

v0:
```python
import math

import jax
import jax.numpy as jnp
from jax import lax
from jax.sharding import PartitionSpec as P

HEADS = 16


epsilon = 1e-06
masked_score = -1e30


def shifted(value, axis, by):
    count = lax.axis_size(axis)
    pairs = [(i, i + by) for i in range(count) if 0 <= i + by < count]
    return lax.ppermute(value, axis, pairs)


def normalize(hidden, gain, shift):
    values = hidden.astype(jnp.float32)
    row_mean = jnp.mean(values, axis=-1, keepdims=True)
    centered = values - row_mean
    variance = jnp.mean(centered * centered, axis=-1, keepdims=True)
    return (centered * lax.rsqrt(variance + epsilon) * gain + shift).astype(jnp.bfloat16)


def per_device(patches, lengths, norm_gain, norm_bias, w_qkv, w_out, out_bias, scale_gain):
    section_index = lax.axis_index("pipe")
    section_count = lax.axis_size("pipe")
    group_count = lax.axis_size("ctx")
    micro_count = patches.shape[0]
    tok_rows = patches.shape[2]
    width = patches.shape[3]
    head_count = HEADS
    head_width = width // head_count
    group_heads = head_count // group_count
    score_scale = head_width ** (-0.5)
    qkv_full = lax.all_gather(w_qkv[0], "dp", axis=1, tiled=True)
    out_full = w_out[0]
    gain = norm_gain[0]
    shift = norm_bias[0]
    out_shift = out_bias[0]
    layer_scale = scale_gain[0]
    turn_count = micro_count + section_count - 1
    received = jnp.zeros((tok_rows, width), jnp.bfloat16)
    results = jnp.zeros((micro_count, tok_rows, width), jnp.bfloat16)
    volume_lengths = lengths[:, 0]
    for turn_index in range(turn_count):
        fresh = patches[min(turn_index, micro_count - 1), 0]
        current = jnp.where(section_index == 0, fresh, received)
        offset_turn = turn_index - section_index
        slot_index = jnp.clip(offset_turn, 0, micro_count - 1)
        length = lax.dynamic_index_in_dim(volume_lengths, slot_index, keepdims=False)
        normed = normalize(current, gain, shift)
        run_projected = jnp.dot(normed, qkv_full, preferred_element_type=jnp.float32).astype(
            jnp.bfloat16
        )
        run_projected = run_projected.reshape(tok_rows, 3, head_count, head_width)
        split_heads = run_projected.reshape(tok_rows, 3, group_count, group_heads, head_width)
        block = lax.all_to_all(split_heads, "ctx", split_axis=2, concat_axis=0, tiled=True)
        queries = block[:, 0, 0]
        key_rows = block[:, 1, 0]
        value_rows = block[:, 2, 0]
        total_rows = key_rows.shape[0]
        local_heads = queries.shape[1]
        valid = jnp.arange(total_rows, dtype=jnp.int32) < length
        query_block = math.gcd(total_rows, 512)
        grouped = queries.reshape(total_rows // query_block, query_block, local_heads, head_width)

        def one_block(query_group):
            scores = (
                jnp.einsum(
                    "qhd,khd->hqk", query_group, key_rows, preferred_element_type=jnp.float32
                )
                * score_scale
            )
            scores = jnp.where(valid[None, None, :], scores, masked_score)
            top_score = jnp.max(scores, axis=-1, keepdims=True)
            weights = jnp.where(valid[None, None, :], jnp.exp(scores - top_score), 0.0)
            totals = jnp.sum(weights, axis=-1)
            context = (
                jnp.einsum(
                    "hqk,khd->qhd",
                    weights.astype(jnp.bfloat16),
                    value_rows,
                    preferred_element_type=jnp.float32,
                )
                / totals.T[:, :, None]
            )
            return context.astype(jnp.bfloat16)

        blocks_out = lax.map(one_block, grouped)
        per_head = blocks_out.reshape(total_rows, 1, local_heads, head_width)
        merged = lax.all_to_all(per_head, "ctx", split_axis=0, concat_axis=1, tiled=True)
        run_context = merged.reshape(tok_rows, head_count, head_width)
        run_context = run_context.reshape(tok_rows, width)
        mixed = jnp.dot(run_context, out_full, preferred_element_type=jnp.float32) + out_shift
        produced = (current.astype(jnp.float32) + layer_scale * mixed).astype(jnp.bfloat16)
        keep_it = (offset_turn >= 0) & (offset_turn < micro_count)
        previous = lax.dynamic_index_in_dim(results, slot_index, keepdims=False)
        results = lax.dynamic_update_index_in_dim(
            results, jnp.where(keep_it, produced, previous), slot_index, 0
        )
        if turn_index + 1 < turn_count:
            received = shifted(produced, "pipe", 1)
    return results[None, :, None]


def solution(mesh):
    in_specs = (
        P(None, "dp", "ctx", None),
        P(None, "dp"),
        P("pipe", None),
        P("pipe", None),
        P("pipe", None, "dp"),
        P("pipe", None, None),
        P("pipe", None),
        P("pipe", None),
    )
    out_specs = P("pipe", None, "dp", "ctx", None)
    return jax.shard_map(
        per_device, mesh=mesh, in_specs=in_specs, out_specs=out_specs, check_vma=False
    )
```

profile of v0, /device:TPU:2, one launch (start us, length us, event | category | flops | bytes accessed | tf_op | source)
XLA Modules:
  0.0 225.3 jit_solution(6807401547627246137)
XLA Ops:
  8.4 1.2 fusion.90
  9.5 116.0 %all-gather.3.cloned.1.call-done = bf16[1,1024,3072]{2,1,0:T(8,128)(2,1)} async-done(((bf16[1,1024,768]{2,1,0:T(8,128)(2,1)}), bf16[1,1024,3072]{2,1,0:T(8,128)(2,1)}) %all-gather.3.cloned.1.call-update) | async-done | bytes 6291472 | tf_op jit(solution)/shard_map/all_gather | solution.py:40
  125.5 4.9 %fusion.6 = bf16[128,3072]{1,0:T(8,128)(2,1)} fusion(bf16[1,1024,3072]{2,1,0:T(8,128)(2,1)} %all-gather.3.cloned.1.call-done, f32[1024]{0:T(1024)} %bitcast.159, f32[1024]{0:T(1024)} %bitcast.161, f32[128]{0:T(128)S(1)} %add_rsqrt_fusion.1, f32[128]{0:T(128)S(1)} %broadcast_multiply_fusion.1, bf16[1,1,128,1024]{3,2,1,0:T(8,128)(2,1)} %param.8, pred[]{:T(512)S(6)} %eq.4), kind=kOutput, calls=%fused_computation.10 | convolution fusion | flops 806617088 | bytes 7349249 | tf_op jit(solution)/shard_map/dot_general | solution.py:57
  130.4 1.5 copy.31
  132.9 3.5 %all-to-all-start = ((bf16[128,3,4,4,64]{0,4,3,1,2:T(8,128)(2,1)}), bf16[128,3,4,4,64]{0,4,3,1,2:T(8,128)(2,1)S(1)}, u32[]{:S(2)}, u32[]{:S(2)}) async-start(bf16[128,3,4,4,64]{0,4,3,1,2:T(8,128)(2,1)} %copy.32), calls=%async_computation | async-start | bytes 1572864 | tf_op jit(solution)/shard_map/all_to_all | solution.py:62
  137.1 11.0 %all-to-all-done = bf16[128,3,4,4,64]{0,4,3,1,2:T(8,128)(2,1)S(1)} async-done(((bf16[128,3,4,4,64]{0,4,3,1,2:T(8,128)(2,1)}), bf16[128,3,4,4,64]{0,4,3,1,2:T(8,128)(2,1)S(1)}, u32[]{:S(2)}, u32[]{:S(2)}) %all-to-all-start) | async-done | bytes 786464 | tf_op jit(solution)/shard_map/all_to_all | solution.py:62
  148.0 1.5 copy.33
  149.6 1.6 all_to_all.51
  151.2 3.3 %fusion.116 = (f32[4,512]{1,0:T(4,128)S(1)}, bf16[4,512,512]{1,2,0:T(8,128)(2,1)}) fusion(pred[512]{0:T(512)(128)(4,1)S(1)} %iota_compare_fusion, bf16[512,3,1,4,64]{0,4,3,2,1:T(8,128)(2,1)S(1)} %all_to_all.51), kind=kOutput, calls=%fused_computation.93 | convolution fusion | flops 140509696 | bytes 2630656 | tf_op jit(solution)/shard_map/while/body/eval_jaxpr/sub | solution.py:81
  154.5 2.1 fusion.73
  157.3 8.4 %all_to_all.66 = bf16[4,2,16384]{2,1,0:T(2,128)(2,1)S(1)} all-to-all(bf16[4,2,16384]{2,1,0:T(2,128)(2,1)S(1)} %reshape.53), channel_id=1, replica_groups=mesh['pipe'=2,'ctx'=4,'dp'=4] {'ctx'}, dimensions={0} | all-to-all | bytes 524288 | tf_op jit(solution)/shard_map/all_to_all | solution.py:96
  167.1 1.3 collective-permute-start
  168.4 8.3 %collective-permute-done = bf16[128,1024]{1,0:T(8,128)(2,1)S(1)} collective-permute-done((bf16[128,1024]{1,0:T(8,128)(2,1)S(1)}, bf16[128,1024]{1,0:T(8,128)(2,1)S(1)}, u32[]{:S(2)}, u32[]{:S(2)}) %collective-permute-start) | collective-permute-done | bytes 262176 | tf_op jit(solution)/shard_map/ppermute | solution.py:18
  177.0 3.9 %fusion.9 = bf16[128,3072]{1,0:T(8,128)(2,1)S(1)} fusion(bf16[1,1024,3072]{2,1,0:T(8,128)(2,1)} %all-gather.3.cloned.1.call-done, bf16[128,1024]{1,0:T(8,128)(2,1)S(1)} %get-tuple-element.28, f32[128]{0:T(128)S(1)} %add_rsqrt_fusion, f32[128]{0:T(128)S(1)} %broadcast_multiply_fusion, f32[1024]{0:T(1024)S(1)} %bitcast.160, f32[1024]{0:T(1024)S(1)} %bitcast.162), kind=kOutput, calls=%fused_computation.11 | convolution fusion | flops 806486016 | bytes 7349248 | tf_op jit(solution)/shard_map/dot_general | solution.py:57
  180.9 1.2 copy.38
  182.1 1.2 copy.39
  183.3 14.1 %all_to_all.67 = bf16[128,3,4,4,64]{0,4,3,1,2:T(8,128)(2,1)S(1)} all-to-all(bf16[128,3,4,4,64]{0,4,3,1,2:T(8,128)(2,1)S(1)} %copy.39), channel_id=1, replica_groups=mesh['pipe'=2,'ctx'=4,'dp'=4] {'ctx'}, dimensions={2} | all-to-all | bytes 1572864 | tf_op jit(solution)/shard_map/all_to_all | solution.py:62
  197.9 1.2 all_to_all.58
  199.2 4.3 %fusion.117 = (f32[4,512]{1,0:T(4,128)S(1)}, bf16[4,512,512]{1,2,0:T(8,128)(2,1)}) fusion(pred[512]{0:T(512)(128)(4,1)S(1)} %iota_compare_fusion, bf16[512,3,1,4,64]{0,4,3,2,1:T(8,128)(2,1)} %all_to_all.58), kind=kOutput, calls=%fused_computation.94 | convolution fusion | flops 140509696 | bytes 2630656 | tf_op jit(solution)/shard_map/while/body/eval_jaxpr/sub | solution.py:81
  203.5 2.2 fusion.70
  206.0 1.1 reshape.55
  207.1 3.4 %all-to-all-start.3 = ((bf16[4,2,16384]{2,1,0:T(2,128)(2,1)}), bf16[4,2,16384]{2,1,0:T(2,128)(2,1)S(1)}, u32[]{:S(2)}, u32[]{:S(2)}) async-start(bf16[4,2,16384]{2,1,0:T(2,128)(2,1)} %reshape.55), calls=%async_computation.3 | async-start | bytes 524288 | tf_op jit(solution)/shard_map/all_to_all | solution.py:96
  210.5 6.0 %all-to-all-done.3 = bf16[4,2,16384]{2,1,0:T(2,128)(2,1)S(1)} async-done(((bf16[4,2,16384]{2,1,0:T(2,128)(2,1)}), bf16[4,2,16384]{2,1,0:T(2,128)(2,1)S(1)}, u32[]{:S(2)}, u32[]{:S(2)}) %all-to-all-start.3) | async-done | bytes 262176 | tf_op jit(solution)/shard_map/all_to_all | solution.py:96
  217.2 1.2 fusion.79
  (34 shorter events, 6.8 us)
Async XLA Ops:
  6.5 160.0 %copy-start = (bf16[1,1024,1024]{2,1,0:T(8,128)(2,1)S(1)}, bf16[1,1024,1024]{2,1,0:T(8,128)(2,1)}, u32[]{:S(2)}) copy-start(bf16[1,1024,1024]{2,1,0:T(8,128)(2,1)} %param.13) | copy-start | bytes 6291460
  6.5 119.0 %all-gather.3.cloned.1.call-start = ((), (), s32[]{:S(2)}) async-start(), calls=%async_computation.4 | async-start | bytes 7864320 | tf_op jit(solution)/shard_map/all_gather | solution.py:40
  132.9 15.1 %all-to-all-start = ((bf16[128,3,4,4,64]{0,4,3,1,2:T(8,128)(2,1)}), bf16[128,3,4,4,64]{0,4,3,1,2:T(8,128)(2,1)S(1)}, u32[]{:S(2)}, u32[]{:S(2)}) async-start(bf16[128,3,4,4,64]{0,4,3,1,2:T(8,128)(2,1)} %copy.32), calls=%async_computation | async-start | bytes 1572864 | tf_op jit(solution)/shard_map/all_to_all | solution.py:62
  154.5 12.0 %copy-start.1 = (bf16[1,1,128,1024]{3,2,1,0:T(8,128)(2,1)S(1)}, bf16[1,1,128,1024]{3,2,1,0:T(8,128)(2,1)}, u32[]{:S(2)}) copy-start(bf16[1,1,128,1024]{3,2,1,0:T(8,128)(2,1)} %param.8) | copy-start | bytes 786436
  154.5 12.1 %copy-start.4 = (f32[1,1024]{1,0:T(1,128)S(1)}, f32[1,1024]{1,0:T(1,128)}, u32[]{:S(2)}) copy-start(f32[1,1024]{1,0:T(1,128)} %param.14) | copy-start | bytes 12292
  154.5 12.1 %copy-start.5 = (f32[1,1024]{1,0:T(1,128)S(1)}, f32[1,1024]{1,0:T(1,128)}, u32[]{:S(2)}) copy-start(f32[1,1024]{1,0:T(1,128)} %param.15) | copy-start | bytes 12292
  156.6 20.4 %copy-start.2 = (f32[1,1024]{1,0:T(1,128)S(1)}, f32[1,1024]{1,0:T(1,128)}, u32[]{:S(2)}) copy-start(f32[1,1024]{1,0:T(1,128)} %param.11) | copy-start | bytes 12292
  156.6 20.4 %copy-start.3 = (f32[1,1024]{1,0:T(1,128)S(1)}, f32[1,1024]{1,0:T(1,128)}, u32[]{:S(2)}) copy-start(f32[1,1024]{1,0:T(1,128)} %param.10) | copy-start | bytes 12292
  167.1 9.6 %collective-permute-start = (bf16[128,1024]{1,0:T(8,128)(2,1)S(1)}, bf16[128,1024]{1,0:T(8,128)(2,1)S(1)}, u32[]{:S(2)}, u32[]{:S(2)}) collective-permute-start(bf16[128,1024]{1,0:T(8,128)(2,1)S(1)} %fusion.61), channel_id=1, source_target_pairs={{0,16},{1,17},{2,18},{3,19},{4,20},{5,21},{6,22},{7,23},{8,24},{9,... | collective-permute-start | bytes 786440 | tf_op jit(solution)/shard_map/ppermute | solution.py:18
  207.1 9.4 %all-to-all-start.3 = ((bf16[4,2,16384]{2,1,0:T(2,128)(2,1)}), bf16[4,2,16384]{2,1,0:T(2,128)(2,1)S(1)}, u32[]{:S(2)}, u32[]{:S(2)}) async-start(bf16[4,2,16384]{2,1,0:T(2,128)(2,1)} %reshape.55), calls=%async_computation.3 | async-start | bytes 524288 | tf_op jit(solution)/shard_map/all_to_all | solution.py:96
Sparse Core Ops, SparseCore 0:
  8.9 116.5 all-gather.2
where the time goes:
time: 226 us; the launch traced here: 225 us
  waiting for transfers between devices  142 us (63%)
  blocking collectives  22.5 us (10%)
  matrix products  22.3 us (10%)
  between operations  14.3 us (6%)
  local copies, waits for them, and re-layouts  13.4 us (6%)
  starting transfers between devices  8.19 us (4%)
  other arithmetic  2.65 us (1%)
    all_gather x1, waiting for transfers between devices, per_device(): qkv_full = lax.all_gather(w_qkv[0], 'dp', axis=1, tiled=True)  116 us
    all_to_all x1, blocking collectives, per_device(): lax.all_to_all(split_heads, 'ctx', split_axis=2, concat_axis=0, tiled=True)  14.1 us
    all_to_all x1, waiting for transfers between devices, per_device(): lax.all_to_all(split_heads, 'ctx', split_axis=2, concat_axis=0, tiled=True)  11 us
    dot_general x2, matrix products, per_device(): jnp.dot(normed, qkv_full, preferred_element_type=jnp.float32)  8.77 us
    all_to_all x1, blocking collectives, per_device(): lax.all_to_all(per_head, 'ctx', split_axis=0, concat_axis=1, tiled=True)  8.42 us
    ppermute x1, waiting for transfers between devices, shifted(): return lax.ppermute(value, axis, pairs)  8.27 us
    sub x2, matrix products, one_block(): weights = jnp.where(valid[None, None, :], jnp.exp(scores - top_score), 0.0)  7.61 us
    all_to_all x1, waiting for transfers between devices, per_device(): lax.all_to_all(per_head, 'ctx', split_axis=0, concat_axis=1, tiled=True)  5.99 us
  transfers between devices with their start and end apart: 4, of which 4 were waited for; matrix products, arithmetic and copies ran while one was open for 1% of the time, Pallas kernels for 0%

commit v1 on v0

--- a/solution.py
+++ b/solution.py
@@ -1,8 +1,11 @@
+import functools
 import math
 
 import jax
 import jax.numpy as jnp
 from jax import lax
+from jax.experimental import pallas as pl
+from jax.experimental.pallas import tpu as pltpu
 from jax.sharding import PartitionSpec as P
 
 HEADS = 16
@@ -108,6 +111,383 @@
     return results[None, :, None]
 
 
+MESH = pl.DeviceIdType.MESH
+PARTS = 3
+DEPTH_CHUNKS = 4
+ROW_CHUNKS = 2
+
+
+def fused_kernel(
+    sizes,
+    length_ref,
+    patches_ref,
+    gain_ref,
+    shift_ref,
+    w_ref,
+    out_w_ref,
+    out_shift_ref,
+    layer_scale_ref,
+    result_ref,
+    hidden,
+    normed,
+    weights,
+    out_w,
+    mine,
+    gathered,
+    w_recv,
+    w_up,
+    w_down,
+    t_send,
+    t_recv,
+    c_send,
+    c_recv,
+    p_send,
+    p_recv,
+    l_sem,
+):
+    rows, width, planes, group = sizes
+    head_width = width // HEADS
+    group_blocks = w_ref.shape[1] // group
+    depth = width // DEPTH_CHUNKS
+    piece = rows // ROW_CHUNKS
+    pairs = group // 128
+    pipe = lax.axis_index("pipe")
+    ctx = lax.axis_index("ctx")
+    plane = lax.axis_index("dp")
+    core, side = ctx % 2, ctx // 2
+    near = side * 2 + (1 - core)
+    across = (1 - side) * 2 + core
+    diagonal = 3 - ctx
+    others = (near, across, diagonal)
+    has_up = plane < planes - 1
+    has_down = plane > 0
+
+    out_w_copy = pltpu.make_async_copy(out_w_ref, out_w, l_sem.at[0])
+    out_w_copy.start()
+
+    def owner_of(part):
+        return (part * 4 + ctx) // group_blocks
+
+    def own_column(part):
+        return pl.multiple_of(((part * 4 + ctx) % group_blocks) * group, group)
+
+    for part in range(PARTS):
+        own_copy = pltpu.make_async_copy(
+            w_ref.at[:, pl.ds(own_column(part), group)], weights.at[part], l_sem.at[1 + part]
+        )
+
+        @pl.when(owner_of(part) == plane)
+        def _(own_copy=own_copy):
+            own_copy.start()
+
+    barrier = pltpu.get_barrier_semaphore()
+    pl.semaphore_signal(barrier, inc=1, device_id={"pipe": 1 - pipe}, device_id_type=MESH)
+    for other in others:
+        pl.semaphore_signal(barrier, inc=1, device_id={"ctx": other}, device_id_type=MESH)
+
+    @pl.when(has_up)
+    def _():
+        pl.semaphore_signal(barrier, inc=1, device_id={"dp": plane + 1}, device_id_type=MESH)
+
+    @pl.when(has_down)
+    def _():
+        pl.semaphore_signal(barrier, inc=1, device_id={"dp": plane - 1}, device_id_type=MESH)
+
+    def normalize_piece(at):
+        span = pl.ds(at * piece, piece)
+        normed[ctx, span, :] = normalize(hidden[span, :], gain_ref[...], shift_ref[...])
+
+    @pl.when(pipe == 0)
+    def _():
+        hidden[...] = patches_ref[...]
+        for at in range(ROW_CHUNKS):
+            normalize_piece(at)
+
+    pl.semaphore_wait(barrier, 4 + has_up.astype(jnp.int32) + has_down.astype(jnp.int32))
+
+    def w_copy(part, at, own, up):
+        span = pl.ds(at * depth, depth)
+        there = weights.at[part, span, :]
+        here = w_ref.at[span, pl.ds(own_column(part), group)] if own else there
+        return pltpu.make_async_remote_copy(
+            src_ref=here,
+            dst_ref=there,
+            send_sem=(w_up if up else w_down).at[part, at],
+            recv_sem=w_recv.at[part, at],
+            device_id={"dp": plane + 1 if up else plane - 1},
+            device_id_type=MESH,
+        )
+
+    for at in range(DEPTH_CHUNKS):
+        for part in range(PARTS):
+            is_own = owner_of(part) == plane
+
+            @pl.when(is_own & has_up)
+            def _(part=part, at=at):
+                w_copy(part, at, True, True).start()
+
+            @pl.when(is_own & has_down)
+            def _(part=part, at=at):
+                w_copy(part, at, True, False).start()
+
+    def t_copy(which, at):
+        whose = across if which == 2 else ctx
+        block = normed.at[whose, pl.ds(at * piece, piece), :]
+        return pltpu.make_async_remote_copy(
+            src_ref=block,
+            dst_ref=block,
+            send_sem=t_send.at[which, at],
+            recv_sem=t_recv.at[which, at],
+            device_id={"ctx": across if which == 1 else near},
+            device_id_type=MESH,
+        )
+
+    def send_piece(at):
+        t_copy(1, at).start()
+        t_copy(0, at).start()
+
+    def pass_pieces():
+        for at in range(ROW_CHUNKS):
+            t_copy(1, at).wait_recv()
+            t_copy(2, at).start()
+
+    @pl.when(pipe == 0)
+    def _():
+        for at in range(ROW_CHUNKS):
+            send_piece(at)
+
+    for at in range(DEPTH_CHUNKS):
+        for part in range(PARTS):
+            owner = owner_of(part)
+
+            @pl.when(owner != plane)
+            def _(part=part, at=at):
+                w_copy(part, at, False, True).wait_recv()
+
+            @pl.when((owner < plane) & has_up)
+            def _(part=part, at=at):
+                w_copy(part, at, False, True).start()
+
+            @pl.when((owner > plane) & has_down)
+            def _(part=part, at=at):
+                w_copy(part, at, False, False).start()
+
+        if at == DEPTH_CHUNKS // 2:
+
+            @pl.when(pipe == 0)
+            def _():
+                pass_pieces()
+
+    def p_copy(at):
+        block = hidden.at[pl.ds(at * piece, piece), :]
+        return pltpu.make_async_remote_copy(
+            src_ref=block,
+            dst_ref=block,
+            send_sem=p_send.at[at],
+            recv_sem=p_recv.at[at],
+            device_id={"pipe": 1 - pipe},
+            device_id_type=MESH,
+        )
+
+    for part in range(PARTS):
+        own_copy = pltpu.make_async_copy(
+            w_ref.at[:, pl.ds(own_column(part), group)], weights.at[part], l_sem.at[1 + part]
+        )
+
+        @pl.when(owner_of(part) == plane)
+        def _(own_copy=own_copy):
+            own_copy.wait()
+
+    @pl.when(pipe == 1)
+    def _():
+        for at in range(ROW_CHUNKS):
+            p_copy(at).wait_recv()
+            normalize_piece(at)
+            send_piece(at)
+        pass_pieces()
+
+    for at in range(ROW_CHUNKS):
+        t_copy(0, at).wait_recv()
+        t_copy(2, at).wait_recv()
+
+    total = 4 * rows
+    tokens = normed[...].reshape(total, width)
+
+    def project(part):
+        return jnp.dot(tokens, weights[part], preferred_element_type=jnp.float32)
+
+    queries = (project(0).astype(jnp.bfloat16) * jnp.bfloat16(head_width**-0.5)).astype(
+        jnp.bfloat16
+    )
+    key_rows = project(1).astype(jnp.bfloat16)
+    value_columns = project(2).T.astype(jnp.bfloat16)
+    key_bias = jnp.where(
+        lax.broadcasted_iota(jnp.int32, (total, 1), 0) < length_ref[0, 0], 0.0, masked_score
+    )
+    lane_head = lax.broadcasted_iota(jnp.int32, (total, 128), 1) // head_width
+
+    def c_copy(other, which, pair):
+        lanes = pl.ds(pair * 128, 128)
+        return pltpu.make_async_remote_copy(
+            src_ref=mine.at[pl.ds(pl.multiple_of(other * rows, rows), rows), lanes],
+            dst_ref=gathered.at[ctx, :, lanes],
+            send_sem=c_send.at[which, pair],
+            recv_sem=c_recv.at[which, pair],
+            device_id={"ctx": other},
+            device_id_type=MESH,
+        )
+
+    per_pair = 128 // head_width
+    for pair in range(pairs):
+        pair_queries = queries[:, pair * 128 : (pair + 1) * 128]
+        pair_keys = key_rows[:, pair * 128 : (pair + 1) * 128]
+        columns = []
+        for head in range(per_pair):
+            head_queries = jnp.where(lane_head == head, pair_queries, jnp.bfloat16(0))
+            scores = lax.dot_general(
+                pair_keys,
+                head_queries,
+                (((1,), (1,)), ((), ())),
+                preferred_element_type=jnp.float32,
+            )
+            scores = scores + key_bias
+            top = jnp.max(scores, axis=0, keepdims=True)
+            exps = jnp.exp(scores - top)
+            totals = jnp.sum(exps, axis=0, keepdims=True)
+            first = (pair * per_pair + head) * head_width
+            part_sum = jnp.dot(
+                value_columns[first : first + head_width, :],
+                exps.astype(jnp.bfloat16),
+                preferred_element_type=jnp.float32,
+            )
+            columns.append(part_sum / totals)
+        context = jnp.concatenate(columns, axis=0).T.astype(jnp.bfloat16)
+        mine[:, pair * 128 : (pair + 1) * 128] = context
+        for which, other in ((1, across), (2, diagonal), (0, near)):
+            c_copy(other, which, pair).start()
+
+    own_rows = pl.ds(pl.multiple_of(ctx * rows, rows), rows)
+    out_w_copy.wait()
+
+    def out_part(block, whose):
+        span = pl.ds(pl.multiple_of(whose * group, group), group)
+        return jnp.dot(block, out_w[span, :], preferred_element_type=jnp.float32)
+
+    mixed = out_part(mine[own_rows, :], ctx)
+    for which, other in enumerate(others):
+        for pair in range(pairs):
+            c_copy(other, which, pair).wait_recv()
+        mixed = mixed + out_part(gathered[other], other)
+    mixed = mixed + out_shift_ref[...]
+    produced = (
+        hidden[...].astype(jnp.float32) + layer_scale_ref[...] * mixed
+    ).astype(jnp.bfloat16)
+    result_ref[...] = produced
+
+    @pl.when(pipe == 0)
+    def _():
+        hidden[...] = produced
+        for at in range(ROW_CHUNKS):
+            p_copy(at).start()
+
+    for at in range(DEPTH_CHUNKS):
+        for part in range(PARTS):
+            owner = owner_of(part)
+
+            @pl.when((owner <= plane) & has_up)
+            def _(part=part, at=at):
+                w_copy(part, at, False, True).wait_send()
+
+            @pl.when((owner >= plane) & has_down)
+            def _(part=part, at=at):
+                w_copy(part, at, False, False).wait_send()
+
+    for at in range(ROW_CHUNKS):
+        for which in range(3):
+            t_copy(which, at).wait_send()
+    for pair in range(pairs):
+        for which, other in enumerate(others):
+            c_copy(other, which, pair).wait_send()
+
+    @pl.when(pipe == 0)
+    def _():
+        for at in range(ROW_CHUNKS):
+            p_copy(at).wait_send()
+
+
+def fused_device(
+    mesh, patches, lengths, norm_gain, norm_bias, w_qkv, w_out, out_bias, scale_gain
+):
+    planes, groups = mesh.shape["dp"], mesh.shape["ctx"]
+    micro_count, _, rows, width = patches.shape
+    group = width // groups
+    fits = (
+        micro_count == 1
+        and mesh.shape["pipe"] == 2
+        and groups == 4
+        and group % 128 == 0
+        and 128 % (width // HEADS) == 0
+        and w_qkv.shape[2] % group == 0
+        and rows % (16 * ROW_CHUNKS) == 0
+        and rows <= 128
+    )
+    if not fits:
+        return per_device(
+            patches, lengths, norm_gain, norm_bias, w_qkv, w_out, out_bias, scale_gain
+        )
+    bf16 = jnp.bfloat16
+    pairs = group // 128
+    vmem = pl.BlockSpec(memory_space=pltpu.VMEM)
+    hbm = pl.BlockSpec(memory_space=pl.ANY)
+    dma = pltpu.SemaphoreType.DMA
+    result = pl.pallas_call(
+        functools.partial(fused_kernel, (rows, width, planes, group)),
+        out_shape=jax.ShapeDtypeStruct((rows, width), bf16),
+        in_specs=[
+            pl.BlockSpec(memory_space=pltpu.SMEM),
+            vmem,
+            vmem,
+            vmem,
+            hbm,
+            hbm,
+            vmem,
+            vmem,
+        ],
+        out_specs=vmem,
+        scratch_shapes=[
+            pltpu.VMEM((rows, width), bf16),
+            pltpu.VMEM((groups, rows, width), bf16),
+            pltpu.VMEM((PARTS, width, group), bf16),
+            pltpu.VMEM((width, width), bf16),
+            pltpu.VMEM((groups * rows, group), bf16),
+            pltpu.VMEM((groups, rows, group), bf16),
+            dma((PARTS, DEPTH_CHUNKS)),
+            dma((PARTS, DEPTH_CHUNKS)),
+            dma((PARTS, DEPTH_CHUNKS)),
+            dma((3, ROW_CHUNKS)),
+            dma((3, ROW_CHUNKS)),
+            dma((3, pairs)),
+            dma((3, pairs)),
+            dma((ROW_CHUNKS,)),
+            dma((ROW_CHUNKS,)),
+            dma((4,)),
+        ],
+        compiler_params=pltpu.CompilerParams(
+            collective_id=0, has_side_effects=True, vmem_limit_bytes=48 * 1024 * 1024
+        ),
+    )(
+        lengths,
+        patches[0, 0],
+        norm_gain,
+        norm_bias,
+        w_qkv[0],
+        w_out[0],
+        out_bias,
+        scale_gain,
+    )
+    return result[None, None, None]
+
+
 def solution(mesh):
     in_specs = (
         P(None, "dp", "ctx", None),
@@ -120,6 +500,7 @@
         P("pipe", None),
     )
     out_specs = P("pipe", None, "dp", "ctx", None)
+    body = functools.partial(fused_device, mesh)
     return jax.shard_map(
-        per_device, mesh=mesh, in_specs=in_specs, out_specs=out_specs, check_vma=False
+        body, mesh=mesh, in_specs=in_specs, out_specs=out_specs, check_vma=False
     )

time: 226 us -> 83.9 us (0.37)
  waiting for transfers between devices: 142 us -> 0 us
  Pallas kernels: 0 us -> 75.5 us
  blocking collectives: 22.5 us -> 0 us
  matrix products: 22.3 us -> 0 us
  between operations: 14.3 us -> 0.67 us
  starting transfers between devices: 8.19 us -> 0 us
  local copies, waits for them, and re-layouts: 13.4 us -> 7.39 us
  other arithmetic: 2.65 us -> 0 us
    all_gather x1 -> x0, waiting for transfers between devices: 116 us -> none  [per_device(): qkv_full = lax.all_gather(w_qkv[0], 'dp', axis=1, tiled=True)]
    pallas_call x0 -> x1, Pallas kernels: none -> 75.5 us  [fused_device(): pl.pallas_call(functools.partial(fused_kernel, (rows, width, planes, grou...]
    all_to_all x2 -> x0, blocking collectives: 22.5 us -> none  [the longest x1 14.1 us: per_device(): lax.all_to_all(split_heads, 'ctx', split_axis=2, concat_axis=0, tiled=True)]
    all_to_all x2 -> x0, waiting for transfers between devices: 17 us -> none  [the longest x1 11 us: per_device(): lax.all_to_all(split_heads, 'ctx', split_axis=2, concat_axis=0, tiled=True)]
    dot_general x6 -> x0, matrix products: 14.7 us -> none  [the longest x2 8.77 us: per_device(): jnp.dot(normed, qkv_full, preferred_element_type=jnp.float32)]
    ppermute x1 -> x0, waiting for transfers between devices: 8.27 us -> none  [shifted(): return lax.ppermute(value, axis, pairs)]
    sub x2 -> x0, matrix products: 7.61 us -> none  [one_block(): weights = jnp.where(valid[None, None, :], jnp.exp(scores - top_score), 0.0)]
    all_to_all x2 -> x0, starting transfers between devices: 6.9 us -> none  [the longest x1 3.49 us: per_device(): lax.all_to_all(split_heads, 'ctx', split_axis=2, concat_axis=0, tiled=True)]
  transfers between devices with their start and end apart: 4 -> 0, of which waited for: 4 -> 0; matrix products, arithmetic and copies ran while one was open for 1% -> 0% of each run, Pallas kernels for 0% -> 0%
where the time goes in v1:
time: 83.9 us; the launch traced here: 83.6 us
  Pallas kernels  75.5 us (90%)
  local copies, waits for them, and re-layouts  7.39 us (9%)
    pallas_call x1, Pallas kernels, fused_device(): pl.pallas_call(functools.partial(fused_kernel, (rows, width, planes, grou...  75.5 us
    unnamed x15, local copies, waits for them, and re-layouts  7.39 us

profile of v1, /device:TPU:2, one launch (start us, length us, event | category | flops | bytes accessed | tf_op | source)
XLA Modules:
  0.0 83.6 jit_solution(15937586847856318960)
XLA Ops:
  0.7 0.0 copy-start
  0.7 1.6 %copy-done = bf16[1,1024,1024]{2,1,0:T(8,128)(2,1)S(1)} copy-done((bf16[1,1024,1024]{2,1,0:T(8,128)(2,1)S(1)}, bf16[1,1024,1024]{2,1,0:T(8,128)(2,1)}, u32[]{:S(2)}) %copy-start) | copy-done | bytes 2097176
  2.2 0.0 copy-start.1
  2.2 1.4 %copy-done.1 = bf16[1,1024,768]{2,1,0:T(8,128)(2,1)S(1)} copy-done((bf16[1,1024,768]{2,1,0:T(8,128)(2,1)S(1)}, bf16[1,1024,768]{2,1,0:T(8,128)(2,1)}, u32[]{:S(2)}) %copy-start.1) | copy-done | bytes 1572888
  3.7 0.0 copy-start.2
  3.7 0.9 %copy-done.2 = bf16[1,1,128,1024]{3,2,1,0:T(8,128)(2,1)S(1)} copy-done((bf16[1,1,128,1024]{3,2,1,0:T(8,128)(2,1)S(1)}, bf16[1,1,128,1024]{3,2,1,0:T(8,128)(2,1)}, u32[]{:S(2)}) %copy-start.2) | copy-done | bytes 262168
  4.6 0.0 copy-start.3
  4.6 0.7 copy-done.3
  5.3 0.0 copy-start.4
  5.3 0.7 copy-done.4
  6.0 0.0 copy-start.5
  6.0 0.7 copy-done.5
  6.7 0.0 copy-start.6
  6.7 0.7 copy-done.6
  7.4 75.5 %shard_map.82 = bf16[128,1024]{1,0:T(8,128)(2,1)S(1)} custom-call(s32[1,1]{1,0:T(1,128)S(6)} %copy.10.length_ref, bf16[128,1024]{1,0:T(8,128)(2,1)S(1)} %bitcast.7, f32[1,1024]{1,0:T(1,128)S(1)} %copy-done.3, f32[1,1024]{1,0:T(1,128)S(1)} %copy-done.4, bf16[1024,768]{1,0:T(8,128)(2,1)S(1)} %bitcast.5, bf16[1024,1024]{1,0:T(8,128)(2,1)S(1)} %bitcast.4, ...), custom_call_target="tpu_custom_call" | custom-call | tf_op jit(solution)/shard_map/pallas_call | solution.py:443
  82.9 0.7 copy.11
Async XLA Ops:
  0.7 1.6 %copy-start = (bf16[1,1024,1024]{2,1,0:T(8,128)(2,1)S(1)}, bf16[1,1024,1024]{2,1,0:T(8,128)(2,1)}, u32[]{:S(2)}) copy-start(bf16[1,1024,1024]{2,1,0:T(8,128)(2,1)} %param.13) | copy-start | bytes 6291460
  2.2 1.4 %copy-start.1 = (bf16[1,1024,768]{2,1,0:T(8,128)(2,1)S(1)}, bf16[1,1024,768]{2,1,0:T(8,128)(2,1)}, u32[]{:S(2)}) copy-start(bf16[1,1024,768]{2,1,0:T(8,128)(2,1)} %param.12) | copy-start | bytes 4718596
  3.7 0.9 %copy-start.2 = (bf16[1,1,128,1024]{3,2,1,0:T(8,128)(2,1)S(1)}, bf16[1,1,128,1024]{3,2,1,0:T(8,128)(2,1)}, u32[]{:S(2)}) copy-start(bf16[1,1,128,1024]{3,2,1,0:T(8,128)(2,1)} %param.8) | copy-start | bytes 786436
  4.6 0.7 copy-start.3
  5.3 0.7 copy-start.4
  6.0 0.7 copy-start.5
  6.7 0.7 copy-start.6

commit v2 on v1

--- a/solution.py
+++ b/solution.py
@@ -113,21 +113,27 @@
 
 MESH = pl.DeviceIdType.MESH
 PARTS = 3
-DEPTH_CHUNKS = 4
-ROW_CHUNKS = 2
+DEPTH_CHUNKS = 8
+SIDE_CHUNKS = 3
+ROW_CHUNKS = 4
 
 
 def fused_kernel(
     sizes,
     length_ref,
     patches_ref,
+    gain_hbm,
+    shift_hbm,
+    w_ref,
+    out_w_ref,
+    out_shift_hbm,
+    layer_scale_hbm,
+    result_ref,
     gain_ref,
     shift_ref,
-    w_ref,
-    out_w_ref,
     out_shift_ref,
     layer_scale_ref,
-    result_ref,
+    side_weights,
     hidden,
     normed,
     weights,
@@ -143,6 +149,10 @@
     c_recv,
     p_send,
     p_recv,
+    b_recv,
+    b_up,
+    b_down,
+    b_cross,
     l_sem,
 ):
     rows, width, planes, group = sizes
@@ -162,6 +172,26 @@
     has_up = plane < planes - 1
     has_down = plane > 0
 
+    direct = DEPTH_CHUNKS - SIDE_CHUNKS
+    patches_copy = pltpu.make_async_copy(patches_ref, hidden, l_sem.at[4])
+
+    @pl.when(pipe == 0)
+    def _():
+        patches_copy.start()
+
+    small_copies = [
+        pltpu.make_async_copy(there, here, l_sem.at[5 + index])
+        for index, (there, here) in enumerate(
+            (
+                (gain_hbm, gain_ref),
+                (shift_hbm, shift_ref),
+                (out_shift_hbm, out_shift_ref),
+                (layer_scale_hbm, layer_scale_ref),
+            )
+        )
+    ]
+    for small_copy in small_copies:
+        small_copy.start()
     out_w_copy = pltpu.make_async_copy(out_w_ref, out_w, l_sem.at[0])
     out_w_copy.start()
 
@@ -197,9 +227,12 @@
         span = pl.ds(at * piece, piece)
         normed[ctx, span, :] = normalize(hidden[span, :], gain_ref[...], shift_ref[...])
 
+    for small_copy in small_copies:
+        small_copy.wait()
+
     @pl.when(pipe == 0)
     def _():
-        hidden[...] = patches_ref[...]
+        patches_copy.wait()
         for at in range(ROW_CHUNKS):
             normalize_piece(at)
 
@@ -218,17 +251,92 @@
             device_id_type=MESH,
         )
 
-    for at in range(DEPTH_CHUNKS):
-        for part in range(PARTS):
-            is_own = owner_of(part) == plane
-
-            @pl.when(is_own & has_up)
-            def _(part=part, at=at):
-                w_copy(part, at, True, True).start()
-
-            @pl.when(is_own & has_down)
-            def _(part=part, at=at):
-                w_copy(part, at, True, False).start()
+    def start_own(part, at):
+        is_own = owner_of(part) == plane
+
+        @pl.when(is_own & has_up)
+        def _():
+            w_copy(part, at, True, True).start()
+
+        @pl.when(is_own & has_down)
+        def _():
+            w_copy(part, at, True, False).start()
+
+    def relay(part, at):
+        owner = owner_of(part)
+
+        @pl.when(owner != plane)
+        def _():
+            w_copy(part, at, False, True).wait_recv()
+
+        @pl.when((owner < plane) & has_up)
+        def _():
+            w_copy(part, at, False, True).start()
+
+        @pl.when((owner > plane) & has_down)
+        def _():
+            w_copy(part, at, False, False).start()
+
+    def cross_in(part, side):
+        span = pl.ds((direct + side) * depth, depth)
+        return pltpu.make_async_remote_copy(
+            src_ref=w_ref.at[span, pl.ds(own_column(part), group)],
+            dst_ref=side_weights.at[part, pl.ds(side * depth, depth), :],
+            send_sem=b_cross.at[part, side],
+            recv_sem=b_recv.at[part, side],
+            device_id={"pipe": 1 - pipe},
+            device_id_type=MESH,
+        )
+
+    def side_copy(part, side, up):
+        block = side_weights.at[part, pl.ds(side * depth, depth), :]
+        return pltpu.make_async_remote_copy(
+            src_ref=block,
+            dst_ref=block,
+            send_sem=(b_up if up else b_down).at[part, side],
+            recv_sem=b_recv.at[part, side],
+            device_id={"dp": plane + 1 if up else plane - 1},
+            device_id_type=MESH,
+        )
+
+    def cross_out(part, side):
+        at = direct + side
+        return pltpu.make_async_remote_copy(
+            src_ref=side_weights.at[part, pl.ds(side * depth, depth), :],
+            dst_ref=weights.at[part, pl.ds(at * depth, depth), :],
+            send_sem=b_cross.at[part, side],
+            recv_sem=w_recv.at[part, at],
+            device_id={"pipe": 1 - pipe},
+            device_id_type=MESH,
+        )
+
+    def relay_side(part, side):
+        owner = owner_of(part)
+        side_copy(part, side, True).wait_recv()
+
+        @pl.when((owner <= plane) & has_up)
+        def _():
+            side_copy(part, side, True).start()
+
+        @pl.when((owner >= plane) & has_down)
+        def _():
+            side_copy(part, side, False).start()
+
+        @pl.when(owner != plane)
+        def _():
+            cross_out(part, side).start()
+
+    @pl.when(pipe == 0)
+    def _():
+        for at in range(direct):
+            for part in range(PARTS):
+                if at < SIDE_CHUNKS:
+
+                    @pl.when(owner_of(part) == plane)
+                    def _(part=part, at=at):
+                        cross_in(part, at).start()
+
+                start_own(part, at)
 
     def t_copy(which, at):
         whose = across if which == 2 else ctx
@@ -255,28 +363,29 @@
     def _():
         for at in range(ROW_CHUNKS):
             send_piece(at)
-
-    for at in range(DEPTH_CHUNKS):
-        for part in range(PARTS):
-            owner = owner_of(part)
-
-            @pl.when(owner != plane)
-            def _(part=part, at=at):
-                w_copy(part, at, False, True).wait_recv()
-
-            @pl.when((owner < plane) & has_up)
-            def _(part=part, at=at):
-                w_copy(part, at, False, True).start()
-
-            @pl.when((owner > plane) & has_down)
-            def _(part=part, at=at):
-                w_copy(part, at, False, False).start()
-
-        if at == DEPTH_CHUNKS // 2:
-
-            @pl.when(pipe == 0)
-            def _():
+        for at in range(direct):
+            for part in range(PARTS):
+                relay(part, at)
+            if at == direct // 2:
                 pass_pieces()
+        for side in range(SIDE_CHUNKS):
+            for part in range(PARTS):
+
+                @pl.when(owner_of(part) != plane)
+                def _(part=part, side=side):
+                    cross_out(part, side).wait_recv()
+
+    @pl.when(pipe == 1)
+    def _():
+        for side in range(SIDE_CHUNKS):
+            for part in range(PARTS):
+                relay_side(part, side)
+        for at in range(DEPTH_CHUNKS):
+            for part in range(PARTS):
+                start_own(part, at)
+        for at in range(DEPTH_CHUNKS):
+            for part in range(PARTS):
+                relay(part, at)
 
     def p_copy(at):
         block = hidden.at[pl.ds(at * piece, piece), :]
@@ -390,17 +499,53 @@
         for at in range(ROW_CHUNKS):
             p_copy(at).start()
 
-    for at in range(DEPTH_CHUNKS):
+    def sent(part, at):
+        owner = owner_of(part)
+
+        @pl.when((owner <= plane) & has_up)
+        def _():
+            w_copy(part, at, False, True).wait_send()
+
+        @pl.when((owner >= plane) & has_down)
+        def _():
+            w_copy(part, at, False, False).wait_send()
+
+    def sent_side(part, side):
+        owner = owner_of(part)
+
+        @pl.when((owner <= plane) & has_up)
+        def _():
+            side_copy(part, side, True).wait_send()
+
+        @pl.when((owner >= plane) & has_down)
+        def _():
+            side_copy(part, side, False).wait_send()
+
+        @pl.when(owner != plane)
+        def _():
+            cross_out(part, side).wait_send()
+
+    for at in range(direct):
         for part in range(PARTS):
-            owner = owner_of(part)
-
-            @pl.when((owner <= plane) & has_up)
-            def _(part=part, at=at):
-                w_copy(part, at, False, True).wait_send()
-
-            @pl.when((owner >= plane) & has_down)
-            def _(part=part, at=at):
-                w_copy(part, at, False, False).wait_send()
+            sent(part, at)
+
+    @pl.when(pipe == 0)
+    def _():
+        for side in range(SIDE_CHUNKS):
+            for part in range(PARTS):
+
+                @pl.when(owner_of(part) == plane)
+                def _(part=part, side=side):
+                    cross_in(part, side).wait_send()
+
+    @pl.when(pipe == 1)
+    def _():
+        for at in range(direct, DEPTH_CHUNKS):
+            for part in range(PARTS):
+                sent(part, at)
+        for side in range(SIDE_CHUNKS):
+            for part in range(PARTS):
+                sent_side(part, side)
 
     for at in range(ROW_CHUNKS):
         for which in range(3):
@@ -445,16 +590,21 @@
         out_shape=jax.ShapeDtypeStruct((rows, width), bf16),
         in_specs=[
             pl.BlockSpec(memory_space=pltpu.SMEM),
-            vmem,
-            vmem,
-            vmem,
             hbm,
             hbm,
-            vmem,
-            vmem,
+            hbm,
+            hbm,
+            hbm,
+            hbm,
+            hbm,
         ],
         out_specs=vmem,
         scratch_shapes=[
+            pltpu.VMEM((1, width), jnp.float32),
+            pltpu.VMEM((1, width), jnp.float32),
+            pltpu.VMEM((1, width), jnp.float32),
+            pltpu.VMEM((1, width), jnp.float32),
+            pltpu.VMEM((PARTS, width // DEPTH_CHUNKS * SIDE_CHUNKS, group), bf16),
             pltpu.VMEM((rows, width), bf16),
             pltpu.VMEM((groups, rows, width), bf16),
             pltpu.VMEM((PARTS, width, group), bf16),
@@ -470,10 +620,14 @@
             dma((3, pairs)),
             dma((ROW_CHUNKS,)),
             dma((ROW_CHUNKS,)),
-            dma((4,)),
+            dma((PARTS, SIDE_CHUNKS)),
+            dma((PARTS, SIDE_CHUNKS)),
+            dma((PARTS, SIDE_CHUNKS)),
+            dma((PARTS, SIDE_CHUNKS)),
+            dma((9,)),
         ],
         compiler_params=pltpu.CompilerParams(
-            collective_id=0, has_side_effects=True, vmem_limit_bytes=48 * 1024 * 1024
+            collective_id=0, has_side_effects=True, vmem_limit_bytes=62 * 1024 * 1024
         ),
     )(
         lengths,

time: 83.9 us -> 145 us (1.73); the launches traced: 83.6 us -> 143 us
  Pallas kernels: 75.5 us -> 141 us
  local copies, waits for them, and re-layouts: 7.39 us -> 1.67 us
    pallas_call x1, Pallas kernels: 75.5 us -> 141 us  [fused_device(): pl.pallas_call(functools.partial(fused_kernel, (rows, width, planes, grou...]
    unnamed x15 -> x1, local copies, waits for them, and re-layouts: 7.39 us -> 1.67 us
where the time goes in v2:
time: 145 us; the launch traced here: 143 us
  Pallas kernels  141 us (97%)
  local copies, waits for them, and re-layouts  1.67 us (1%)
    pallas_call x1, Pallas kernels, fused_device(): pl.pallas_call(functools.partial(fused_kernel, (rows, width, planes, grou...  141 us

profile of v2, /device:TPU:2, one launch (start us, length us, event | category | flops | bytes accessed | tf_op | source)
XLA Modules:
  0.0 143.3 jit_solution(14489255147312273795)
XLA Ops:
  0.7 140.9 %shard_map.82 = bf16[128,1024]{1,0:T(8,128)(2,1)} custom-call(s32[1,1]{1,0:T(1,128)S(6)} %copy.10.length_ref, bf16[128,1024]{1,0:T(8,128)(2,1)} %bitcast.7, f32[1,1024]{1,0:T(1,128)} %gain_hbm.1, f32[1,1024]{1,0:T(1,128)} %shift_hbm.1, bf16[1024,768]{1,0:T(8,128)(2,1)} %bitcast.5, bf16[1024,1024]{1,0:T(8,128)(2,1)} %bitcast.4, f32[1,1024]{1,0:T(1,128)} %out_shift_hbm.1, ...), custom_call_target="tpu_custom_call" | custom-call | tf_op jit(solution)/shard_map/pallas_call | solution.py:588
  141.6 1.7 %copy.11 = bf16[1,1,1,128,1024]{4,3,2,1,0:T(8,128)(2,1)} copy(bf16[1,1,1,128,1024]{4,3,2,1,0:T(8,128)(2,1)} %bitcast.6) | data formatting | bytes 524288

commit v3 on v2

--- a/solution.py
+++ b/solution.py
@@ -113,9 +113,9 @@
 
 MESH = pl.DeviceIdType.MESH
 PARTS = 3
-DEPTH_CHUNKS = 8
-SIDE_CHUNKS = 3
-ROW_CHUNKS = 4
+DEPTH_CHUNKS = 4
+SIDE_CHUNKS = 1
+ROW_CHUNKS = 2
 
 
 def fused_kernel(
@@ -236,14 +236,22 @@
         for at in range(ROW_CHUNKS):
             normalize_piece(at)
 
+    for part in range(PARTS):
+        own_copy = pltpu.make_async_copy(
+            w_ref.at[:, pl.ds(own_column(part), group)], weights.at[part], l_sem.at[1 + part]
+        )
+
+        @pl.when(owner_of(part) == plane)
+        def _(own_copy=own_copy):
+            own_copy.wait()
+
     pl.semaphore_wait(barrier, 4 + has_up.astype(jnp.int32) + has_down.astype(jnp.int32))
 
-    def w_copy(part, at, own, up):
+    def w_copy(part, at, up):
         span = pl.ds(at * depth, depth)
         there = weights.at[part, span, :]
-        here = w_ref.at[span, pl.ds(own_column(part), group)] if own else there
         return pltpu.make_async_remote_copy(
-            src_ref=here,
+            src_ref=there,
             dst_ref=there,
             send_sem=(w_up if up else w_down).at[part, at],
             recv_sem=w_recv.at[part, at],
@@ -256,31 +264,31 @@
 
         @pl.when(is_own & has_up)
         def _():
-            w_copy(part, at, True, True).start()
+            w_copy(part, at, True).start()
 
         @pl.when(is_own & has_down)
         def _():
-            w_copy(part, at, True, False).start()
+            w_copy(part, at, False).start()
 
     def relay(part, at):
         owner = owner_of(part)
 
         @pl.when(owner != plane)
         def _():
-            w_copy(part, at, False, True).wait_recv()
+            w_copy(part, at, True).wait_recv()
 
         @pl.when((owner < plane) & has_up)
         def _():
-            w_copy(part, at, False, True).start()
+            w_copy(part, at, True).start()
 
         @pl.when((owner > plane) & has_down)
         def _():
-            w_copy(part, at, False, False).start()
+            w_copy(part, at, False).start()
 
     def cross_in(part, side):
         span = pl.ds((direct + side) * depth, depth)
         return pltpu.make_async_remote_copy(
-            src_ref=w_ref.at[span, pl.ds(own_column(part), group)],
+            src_ref=weights.at[part, span, :],
             dst_ref=side_weights.at[part, pl.ds(side * depth, depth), :],
             send_sem=b_cross.at[part, side],
             recv_sem=b_recv.at[part, side],
@@ -397,15 +405,6 @@
             device_id={"pipe": 1 - pipe},
             device_id_type=MESH,
         )
-
-    for part in range(PARTS):
-        own_copy = pltpu.make_async_copy(
-            w_ref.at[:, pl.ds(own_column(part), group)], weights.at[part], l_sem.at[1 + part]
-        )
-
-        @pl.when(owner_of(part) == plane)
-        def _(own_copy=own_copy):
-            own_copy.wait()
 
     @pl.when(pipe == 1)
     def _():
@@ -504,11 +503,11 @@
 
         @pl.when((owner <= plane) & has_up)
         def _():
-            w_copy(part, at, False, True).wait_send()
+            w_copy(part, at, True).wait_send()
 
         @pl.when((owner >= plane) & has_down)
         def _():
-            w_copy(part, at, False, False).wait_send()
+            w_copy(part, at, False).wait_send()
 
     def sent_side(part, side):
         owner = owner_of(part)

time: 145 us -> 92.2 us (0.64)
  the two profiles are of different devices: /device:TPU:2 before, /device:TPU:6 now
where the time goes in v3:
time: 92.2 us; the launch traced here: 92 us
  Pallas kernels  89.7 us (97%)
  local copies, waits for them, and re-layouts  1.67 us (2%)
    pallas_call x1, Pallas kernels, fused_device(): pl.pallas_call(functools.partial(fused_kernel, (rows, width, planes, grou...  89.7 us

profile of v3, /device:TPU:6, one launch (start us, length us, event | category | flops | bytes accessed | tf_op | source)
XLA Modules:
  0.0 92.0 jit_solution(14565393920748289153)
XLA Ops:
  0.7 89.7 %shard_map.82 = bf16[128,1024]{1,0:T(8,128)(2,1)} custom-call(s32[1,1]{1,0:T(1,128)S(6)} %copy.10.length_ref, bf16[128,1024]{1,0:T(8,128)(2,1)} %bitcast.7, f32[1,1024]{1,0:T(1,128)} %gain_hbm.1, f32[1,1024]{1,0:T(1,128)} %shift_hbm.1, bf16[1024,768]{1,0:T(8,128)(2,1)} %bitcast.5, bf16[1024,1024]{1,0:T(8,128)(2,1)} %bitcast.4, f32[1,1024]{1,0:T(1,128)} %out_shift_hbm.1, ...), custom_call_target="tpu_custom_call" | custom-call | tf_op jit(solution)/shard_map/pallas_call | solution.py:587
  90.3 1.7 %copy.11 = bf16[1,1,1,128,1024]{4,3,2,1,0:T(8,128)(2,1)} copy(bf16[1,1,1,128,1024]{4,3,2,1,0:T(8,128)(2,1)} %bitcast.6) | data formatting | bytes 524288

commit v4 on v3

--- a/solution.py
+++ b/solution.py
@@ -285,6 +285,17 @@
         def _():
             w_copy(part, at, False).start()
 
+    def distance(part):
+        return jnp.abs(owner_of(part) - plane)
+
+    def relay_from(away, count):
+        for at in range(count):
+            for part in range(PARTS):
+
+                @pl.when(distance(part) == away)
+                def _(part=part, at=at):
+                    relay(part, at)
+
     def cross_in(part, side):
         span = pl.ds((direct + side) * depth, depth)
         return pltpu.make_async_remote_copy(
@@ -371,10 +382,9 @@
     def _():
         for at in range(ROW_CHUNKS):
             send_piece(at)
-        for at in range(direct):
-            for part in range(PARTS):
-                relay(part, at)
-            if at == direct // 2:
+        for away in range(1, planes):
+            relay_from(away, direct)
+            if away == 1:
                 pass_pieces()
         for side in range(SIDE_CHUNKS):
             for part in range(PARTS):
@@ -385,15 +395,22 @@
 
     @pl.when(pipe == 1)
     def _():
-        for side in range(SIDE_CHUNKS):
-            for part in range(PARTS):
-                relay_side(part, side)
-        for at in range(DEPTH_CHUNKS):
+        for away in range(planes):
+            for side in range(SIDE_CHUNKS):
+                for part in range(PARTS):
+
+                    @pl.when(distance(part) == away)
+                    def _(part=part, side=side):
+                        relay_side(part, side)
+
+            if away < 2:
+                for part in range(PARTS):
+                    start_own(part, away)
+        for at in range(2, DEPTH_CHUNKS):
             for part in range(PARTS):
                 start_own(part, at)
-        for at in range(DEPTH_CHUNKS):
-            for part in range(PARTS):
-                relay(part, at)
+        for away in range(1, planes):
+            relay_from(away, DEPTH_CHUNKS)
 
     def p_copy(at):
         block = hidden.at[pl.ds(at * piece, piece), :]

time: 92.2 us -> 63.4 us (0.69)
  Pallas kernels: 89.7 us -> 60.9 us
    pallas_call x1, Pallas kernels: 89.7 us -> 60.9 us  [fused_device(): pl.pallas_call(functools.partial(fused_kernel, (rows, width, planes, grou...]
where the time goes in v4:
time: 63.4 us; the launch traced here: 63.2 us
  Pallas kernels  60.9 us (96%)
  local copies, waits for them, and re-layouts  1.67 us (3%)
  between operations  0.66 us (1%)
    pallas_call x1, Pallas kernels, fused_device(): pl.pallas_call(functools.partial(fused_kernel, (rows, width, planes, grou...  60.9 us
    unnamed x1, local copies, waits for them, and re-layouts  1.67 us

profile of v4, /device:TPU:6, one launch (start us, length us, event | category | flops | bytes accessed | tf_op | source)
XLA Modules:
  0.0 63.2 jit_solution(10044537154521535846)
XLA Ops:
  0.7 60.9 %shard_map.82 = bf16[128,1024]{1,0:T(8,128)(2,1)} custom-call(s32[1,1]{1,0:T(1,128)S(6)} %copy.10.length_ref, bf16[128,1024]{1,0:T(8,128)(2,1)} %bitcast.7, f32[1,1024]{1,0:T(1,128)} %gain_hbm.1, f32[1,1024]{1,0:T(1,128)} %shift_hbm.1, bf16[1024,768]{1,0:T(8,128)(2,1)} %bitcast.5, bf16[1024,1024]{1,0:T(8,128)(2,1)} %bitcast.4, f32[1,1024]{1,0:T(1,128)} %out_shift_hbm.1, ...), custom_call_target="tpu_custom_call" | custom-call | tf_op jit(solution)/shard_map/pallas_call | solution.py:604
  61.5 1.7 %copy.11 = bf16[1,1,1,128,1024]{4,3,2,1,0:T(8,128)(2,1)} copy(bf16[1,1,1,128,1024]{4,3,2,1,0:T(8,128)(2,1)} %bitcast.6) | data formatting | bytes 524288

commit v5 on v4

--- a/solution.py
+++ b/solution.py
@@ -273,17 +273,22 @@
     def relay(part, at):
         owner = owner_of(part)
 
-        @pl.when(owner != plane)
+        @pl.when((owner < plane) & has_up)
         def _():
             w_copy(part, at, True).wait_recv()
-
-        @pl.when((owner < plane) & has_up)
-        def _():
             w_copy(part, at, True).start()
 
         @pl.when((owner > plane) & has_down)
         def _():
+            w_copy(part, at, False).wait_recv()
             w_copy(part, at, False).start()
+
+    def arrive(part, at):
+        owner = owner_of(part)
+
+        @pl.when(((owner < plane) & (plane == planes - 1)) | ((owner > plane) & (plane == 0)))
+        def _():
+            w_copy(part, at, True).wait_recv()
 
     def distance(part):
         return jnp.abs(owner_of(part) - plane)
@@ -386,13 +391,6 @@
             relay_from(away, direct)
             if away == 1:
                 pass_pieces()
-        for side in range(SIDE_CHUNKS):
-            for part in range(PARTS):
-
-                @pl.when(owner_of(part) != plane)
-                def _(part=part, side=side):
-                    cross_out(part, side).wait_recv()
-
     @pl.when(pipe == 1)
     def _():
         for away in range(planes):
@@ -434,6 +432,25 @@
     for at in range(ROW_CHUNKS):
         t_copy(0, at).wait_recv()
         t_copy(2, at).wait_recv()
+
+    for at in range(direct):
+        for part in range(PARTS):
+            arrive(part, at)
+
+    @pl.when(pipe == 0)
+    def _():
+        for side in range(SIDE_CHUNKS):
+            for part in range(PARTS):
+
+                @pl.when(owner_of(part) != plane)
+                def _(part=part, side=side):
+                    cross_out(part, side).wait_recv()
+
+    @pl.when(pipe == 1)
+    def _():
+        for at in range(direct, DEPTH_CHUNKS):
+            for part in range(PARTS):
+                arrive(part, at)
 
     total = 4 * rows
     tokens = normed[...].reshape(total, width)

time: 63.4 us -> 60 us (0.946)
  the two profiles are of different devices: /device:TPU:6 before, /device:TPU:2 now
where the time goes in v5:
time: 60 us; the launch traced here: 59.8 us
  Pallas kernels  57.4 us (96%)
  local copies, waits for them, and re-layouts  1.67 us (3%)
  between operations  0.66 us (1%)
    pallas_call x1, Pallas kernels, fused_device(): pl.pallas_call(functools.partial(fused_kernel, (rows, width, planes, grou...  57.4 us
    unnamed x1, local copies, waits for them, and re-layouts  1.67 us

profile of v5, /device:TPU:2, one launch (start us, length us, event | category | flops | bytes accessed | tf_op | source)
XLA Modules:
  0.0 59.8 jit_solution(5704994233808253914)
XLA Ops:
  0.7 57.4 %shard_map.82 = bf16[128,1024]{1,0:T(8,128)(2,1)} custom-call(s32[1,1]{1,0:T(1,128)S(6)} %copy.10.length_ref, bf16[128,1024]{1,0:T(8,128)(2,1)} %bitcast.7, f32[1,1024]{1,0:T(1,128)} %gain_hbm.1, f32[1,1024]{1,0:T(1,128)} %shift_hbm.1, bf16[1024,768]{1,0:T(8,128)(2,1)} %bitcast.5, bf16[1024,1024]{1,0:T(8,128)(2,1)} %bitcast.4, f32[1,1024]{1,0:T(1,128)} %out_shift_hbm.1, ...), custom_call_target="tpu_custom_call" | custom-call | tf_op jit(solution)/shard_map/pallas_call | solution.py:621
  58.1 1.7 %copy.11 = bf16[1,1,1,128,1024]{4,3,2,1,0:T(8,128)(2,1)} copy(bf16[1,1,1,128,1024]{4,3,2,1,0:T(8,128)(2,1)} %bitcast.6) | data formatting | bytes 524288

commit v6 on v5

--- a/solution.py
+++ b/solution.py
@@ -115,7 +115,7 @@
 PARTS = 3
 DEPTH_CHUNKS = 4
 SIDE_CHUNKS = 1
-ROW_CHUNKS = 2
+ROW_CHUNKS = 4
 
 
 def fused_kernel(

time: 60 us -> 58.9 us (0.982)
  Pallas kernels: 57.4 us -> 56.4 us
    pallas_call x1, Pallas kernels: 57.4 us -> 56.4 us  [fused_device(): pl.pallas_call(functools.partial(fused_kernel, (rows, width, planes, grou...]
where the time goes in v6:
time: 58.9 us; the launch traced here: 58.8 us
  Pallas kernels  56.4 us (96%)
  local copies, waits for them, and re-layouts  1.67 us (3%)
  between operations  0.66 us (1%)
    pallas_call x1, Pallas kernels, fused_device(): pl.pallas_call(functools.partial(fused_kernel, (rows, width, planes, grou...  56.4 us
    unnamed x1, local copies, waits for them, and re-layouts  1.67 us

profile of v6, /device:TPU:2, one launch (start us, length us, event | category | flops | bytes accessed | tf_op | source)
XLA Modules:
  0.0 58.8 jit_solution(5327524258123627864)
XLA Ops:
  0.7 56.4 %shard_map.82 = bf16[128,1024]{1,0:T(8,128)(2,1)} custom-call(s32[1,1]{1,0:T(1,128)S(6)} %copy.10.length_ref, bf16[128,1024]{1,0:T(8,128)(2,1)} %bitcast.7, f32[1,1024]{1,0:T(1,128)} %gain_hbm.1, f32[1,1024]{1,0:T(1,128)} %shift_hbm.1, bf16[1024,768]{1,0:T(8,128)(2,1)} %bitcast.5, bf16[1024,1024]{1,0:T(8,128)(2,1)} %bitcast.4, f32[1,1024]{1,0:T(1,128)} %out_shift_hbm.1, ...), custom_call_target="tpu_custom_call" | custom-call | tf_op jit(solution)/shard_map/pallas_call | solution.py:621
  57.1 1.7 %copy.11 = bf16[1,1,1,128,1024]{4,3,2,1,0:T(8,128)(2,1)} copy(bf16[1,1,1,128,1024]{4,3,2,1,0:T(8,128)(2,1)} %bitcast.6) | data formatting | bytes 524288
